TPU v7x, 256 devices: a whole 4x4x8 slice. The times are simulated.
256 devices in a mesh: dp: 256 (over x, z, y, core).
Axes of the slice: x: 4, y: 4, z: 8, core: 2. Of those that a mesh axis runs over, the one named last changes fastest.
Arguments:
- picture_embedding_unscaled: bfloat16 [262144, 1152], P('dp'), may hold values from -6 to 6
- caption_embedding_unscaled: bfloat16 [262144, 1152], P('dp'), may hold values from -6 to 6
- score_multiplier: float32 [1], replicated, may hold values from 5 to 15
- score_shift_term_array: float32 [1], replicated, may hold values from -4 to -1
Outputs:
- row_loss: float32 [262144], P('dp')
- image_grad: bfloat16 [262144, 1152], P('dp')
- text_grad: bfloat16 [262144, 1152], P('dp')
All inputs are finite; a program needn't handle non-finite values.
Results may differ from a plain program's by a relative error of at most 0.0061.
Values may be sent and summed in bfloat16 or wider, within the bound.
A program may use at most 64 MiB of HBM per device.

v0:
```python
import jax
import jax.numpy as jnp
from jax import lax
from jax.sharding import PartitionSpec as P

ROUNDS = 2


def passed_along(block, axis, distance):
    devices = range(lax.axis_size(axis))
    route = [((i - distance) % len(devices), i) for i in devices]
    return lax.ppermute(block, axis, route)


def normalize(values):
    wide = values.astype(jnp.float32)
    size = jnp.sqrt(jnp.sum(wide * wide, axis=-1, keepdims=True) + 1e-06)
    return (wide / size, size)


def tile_penalty_parts(
    preceding_device,
    following_device,
    score_multiplier,
    score_shift_term_array,
    matching_index_filter,
):
    inner_similarity = jnp.einsum(
        "id,jd->ij", preceding_device, following_device, preferred_element_type=jnp.float32
    )
    couple_scores = score_multiplier[0] * inner_similarity + score_shift_term_array[0]
    if matching_index_filter:
        rows = lax.broadcasted_iota(jnp.int32, couple_scores.shape, 0)
        cols = lax.broadcasted_iota(jnp.int32, couple_scores.shape, 1)
        target_polarity = jnp.where(rows == cols, 1.0, -1.0).astype(jnp.float32)
    else:
        target_polarity = jnp.full(couple_scores.shape, -1.0, jnp.float32)
    loss_values = jnp.sum(jax.nn.softplus(-target_polarity * couple_scores), axis=1)
    derivative_multiplier = (
        -target_polarity * jax.nn.sigmoid(-target_polarity * couple_scores) * score_multiplier[0]
    ).astype(jnp.bfloat16)
    return (loss_values, derivative_multiplier)


def unit_backward(grad, unit, size):
    along = jnp.sum(unit * grad, axis=-1, keepdims=True)
    return ((grad - unit * along) / size).astype(jnp.bfloat16)


def shards(
    picture_embedding_unscaled, caption_embedding_unscaled, score_multiplier, score_shift_term_array
):
    rounds = ROUNDS
    pairs = picture_embedding_unscaled.shape[0]
    image_unit, image_size = normalize(picture_embedding_unscaled)
    text_unit, text_size = normalize(caption_embedding_unscaled)
    picture_summed_share = image_unit.astype(jnp.bfloat16)
    caption_summed_share = text_unit.astype(jnp.bfloat16)
    loss_values, derivative_multiplier = tile_penalty_parts(
        picture_summed_share, caption_summed_share, score_multiplier, score_shift_term_array, True
    )
    image_acc = jnp.dot(
        derivative_multiplier, caption_summed_share, preferred_element_type=jnp.float32
    )
    text_acc = jnp.einsum(
        "ij,id->jd", derivative_multiplier, picture_summed_share, preferred_element_type=jnp.float32
    )
    counterpart_slice = caption_summed_share
    counterpart_slice = passed_along(counterpart_slice, "dp", 1)
    line_penalty_parts, derivative_multiplier = tile_penalty_parts(
        picture_summed_share, counterpart_slice, score_multiplier, score_shift_term_array, False
    )
    loss_values = loss_values + line_penalty_parts
    image_acc = image_acc + jnp.dot(
        derivative_multiplier, counterpart_slice, preferred_element_type=jnp.float32
    )
    partial_grad = jnp.einsum(
        "ij,id->jd", derivative_multiplier, picture_summed_share, preferred_element_type=jnp.float32
    )
    returned = passed_along(partial_grad.astype(jnp.bfloat16), "dp", -1)
    text_acc = text_acc + returned.astype(jnp.float32)
    row_loss = loss_values / (rounds * pairs)
    image_grad = unit_backward(image_acc, image_unit, image_size)
    text_grad = unit_backward(text_acc, text_unit, text_size)
    return (row_loss, image_grad, text_grad)


def solution(mesh):
    in_specs = (P("dp", None), P("dp", None), P(), P())
    out_specs = (P("dp"), P("dp", None), P("dp", None))
    return jax.shard_map(shards, mesh=mesh, in_specs=in_specs, out_specs=out_specs, check_vma=False)
```

profile of v0, /device:TPU:0, one launch (start us, length us, event | category | flops | bytes accessed | tf_op | source)
XLA Modules:
  0.0 81.5 jit_solution(3930532693879663411)
XLA Ops:
  0.6 0.0 copy-start.1
  0.6 2.3 %fusion.1 = f32[1024]{0:T(1024)S(1)} fusion(bf16[1024,1152]{1,0:T(8,128)(2,1)} %param.5), kind=kLoop, calls=%fused_computation.7 | loop fusion | flops 3537920 | bytes 2363392 | tf_op jit(solution)/shard_map/reduce_sum | solution.py:17
  3.0 2.4 %fusion.5 = bf16[1024,1152]{1,0:T(8,128)(2,1)S(1)} fusion(f32[1024]{0:T(1024)S(1)} %add_sqrt_fusion, bf16[1024,1152]{1,0:T(8,128)(2,1)} %param.5), kind=kLoop, calls=%fused_computation.27 | loop fusion | flops 3538944 | bytes 4722688 | tf_op jit(solution)/shard_map/convert_element_type | solution.py:58
  5.4 0.1 collective-permute-start
  6.8 0.0 copy-done.1
  6.8 0.5 fusion
  7.4 7.5 %multiply_convert_fusion.1 = (bf16[1024,1024]{0,1:T(8,128)(2,1)S(1)}, f32[1024]{0:T(1024)S(1)}) fusion(f32[]{:T(128)} %bitcast.12, f32[]{:T(128)} %bitcast.10, bf16[1024,1152]{1,0:T(8,128)(2,1)S(1)} %fusion.5, f32[1024]{0:T(1024)S(1)} %add_sqrt_fusion.1, bf16[1024,1152]{1,0:T(8,128)(2,1)S(1)} %copy-done.1), kind=kOutput, calls=%fused_computation.17 | convolution fusion | flops 2439379968 | bytes 6823944 | tf_op jit(solution)/shard_map/id,jd->ij/dot_general | solution.py:28
  14.9 3.0 %fusion.13 = f32[1024,1152]{1,0:T(8,128)S(1)} fusion(bf16[1024,1024]{0,1:T(8,128)(2,1)S(1)} %get-tuple-element.3, bf16[1024,1152]{1,0:T(8,128)(2,1)S(1)} %fusion.5), kind=kOutput, calls=%fused_computation.31 | convolution fusion | flops 2415919104 | bytes 9175040 | tf_op jit(solution)/shard_map/dot_general | solution.py:62
  17.9 22.3 %collective-permute-done = bf16[1024,1152]{1,0:T(8,128)(2,1)S(1)} collective-permute-done((bf16[1024,1152]{1,0:T(8,128)(2,1)S(1)}, bf16[1024,1152]{1,0:T(8,128)(2,1)S(1)}, u32[]{:S(2)}, u32[]{:S(2)}) %collective-permute-start) | collective-permute-done | bytes 2359328 | tf_op jit(solution)/shard_map/ppermute | solution.py:12
  40.2 4.9 %fusion.3 = (f32[1024]{0:T(1024)S(1)}, f32[1024,1024]{0,1:T(8,128)S(1)}) fusion(f32[]{:T(128)} %bitcast.14, f32[]{:T(128)} %bitcast.11, bf16[1024,1152]{1,0:T(8,128)(2,1)S(1)} %collective-permute-done, f32[1024]{0:T(1024)S(1)} %add_sqrt_fusion.1, bf16[1024,1152]{1,0:T(8,128)(2,1)S(1)} %copy-done.1), kind=kOutput, calls=%fused_computation.15 | convolution fusion | flops 2428894208 | bytes 8921096 | tf_op jit(solution)/shard_map/id,jd->ij/dot_general | solution.py:28
  45.2 3.6 %convolution_convert_fusion = bf16[1024,1152]{1,0:T(8,128)(2,1)S(1)} fusion(f32[1024,1024]{0,1:T(8,128)S(1)} %get-tuple-element.6, f32[]{:T(128)} %bitcast.13, f32[]{:T(128)} %bitcast.8, f32[1024]{0:T(1024)S(1)} %add_sqrt_fusion.1, bf16[1024,1152]{1,0:T(8,128)(2,1)S(1)} %copy-done.1), kind=kOutput, calls=%fused_computation.22 | convolution fusion | flops 2427977728 | bytes 8917000 | tf_op jit(solution)/shard_map/ij,id->jd/dot_general | solution.py:77
  48.8 0.3 collective-permute-start.1
  49.1 3.8 %multiply_reduce_fusion.1 = (f32[1024]{0:T(1024)S(1)}, f32[1024,1152]{1,0:T(8,128)S(1)}) fusion(f32[1024]{0:T(1024)S(1)} %add_sqrt_fusion.1, bf16[1024,1152]{1,0:T(8,128)(2,1)S(1)} %copy-done.1, f32[1024,1152]{1,0:T(8,128)S(1)} %fusion.13, bf16[1024,1152]{1,0:T(8,128)(2,1)S(1)} %collective-permute-done, f32[1024,1024]{0,1:T(8,128)S(1)} %get-tuple-element.6, ...), kind=kOutput, calls=%fused_computation.12 | convolution fusion | flops 2429156352 | bytes 18358280 | tf_op jit(solution)/shard_map/dot_general | solution.py:74
  52.9 0.6 add_multiply_fusion.1
  53.5 0.0 copy-start
  53.5 2.2 %divide_convert_fusion.1 = bf16[1024,1152]{1,0:T(8,128)(2,1)} fusion(f32[1024,1152]{1,0:T(8,128)S(1)} %get-tuple-element.8, f32[1024]{0:T(1024)S(1)} %get-tuple-element.7, f32[1024]{0:T(1024)S(1)} %add_sqrt_fusion.1, bf16[1024,1152]{1,0:T(8,128)(2,1)S(1)} %copy-done.1), kind=kLoop, calls=%fused_computation.11 | loop fusion | flops 7077888 | bytes 9445376 | tf_op jit(solution)/shard_map/convert_element_type | solution.py:47
  55.7 19.8 %collective-permute-done.1 = bf16[1024,1152]{1,0:T(8,128)(2,1)S(1)} collective-permute-done((bf16[1024,1152]{1,0:T(8,128)(2,1)S(1)}, bf16[1024,1152]{1,0:T(8,128)(2,1)S(1)}, u32[]{:S(2)}, u32[]{:S(2)}) %collective-permute-start.1) | collective-permute-done | bytes 2359328 | tf_op jit(solution)/shard_map/ppermute | solution.py:12
  75.5 0.0 copy-done
  75.5 3.4 %multiply_reduce_fusion = (f32[1024]{0:T(1024)S(1)}, f32[1024,1152]{1,0:T(8,128)S(1)}) fusion(bf16[1024,1152]{1,0:T(8,128)(2,1)S(1)} %collective-permute-done.1, f32[1024]{0:T(1024)S(1)} %add_sqrt_fusion, bf16[1024,1152]{1,0:T(8,128)(2,1)S(1)} %copy-done, bf16[1024,1024]{0,1:T(8,128)(2,1)S(1)} %get-tuple-element.3, f32[1024]{0:T(1024)S(1)} %add_sqrt_fusion.1, ...), kind=kOutput, calls=%fused_computation.9 | convolution fusion | flops 2426534912 | bytes 13905920 | tf_op jit(solution)/shard_map/ij,id->jd/dot_general | solution.py:65
  78.9 2.6 %divide_convert_fusion = bf16[1024,1152]{1,0:T(8,128)(2,1)} fusion(f32[1024,1152]{1,0:T(8,128)S(1)} %get-tuple-element.10, bf16[1024,1152]{1,0:T(8,128)(2,1)S(1)} %collective-permute-done.1, f32[1024]{0:T(1024)S(1)} %get-tuple-element.9, f32[1024]{0:T(1024)S(1)} %add_sqrt_fusion, bf16[1024,1152]{1,0:T(8,128)(2,1)S(1)} %copy-done), kind=kLoop, calls=%fused_computation.8 | loop fusion | flops 9437184 | bytes 11804672 | tf_op jit(solution)/shard_map/convert_element_type | solution.py:47
  (2 shorter events, 0.0 us)
Async XLA Ops:
  0.6 6.2 %copy-start.1 = (bf16[1024,1152]{1,0:T(8,128)(2,1)S(1)}, bf16[1024,1152]{1,0:T(8,128)(2,1)}, u32[]{:S(2)}) copy-start(bf16[1024,1152]{1,0:T(8,128)(2,1)} %param.4) | copy-start | bytes 7077892
  5.4 34.8 %collective-permute-start = (bf16[1024,1152]{1,0:T(8,128)(2,1)S(1)}, bf16[1024,1152]{1,0:T(8,128)(2,1)S(1)}, u32[]{:S(2)}, u32[]{:S(2)}) collective-permute-start(bf16[1024,1152]{1,0:T(8,128)(2,1)S(1)} %fusion.5), channel_id=1, source_target_pairs={{255,0},{0,1},{1,2},{2,3},{3,4},{4,5},{5,6},{6,7},{7,8},{8,9},{9,1... | collective-permute-start | bytes 7077896 | tf_op jit(solution)/shard_map/ppermute | solution.py:12
  48.8 26.7 %collective-permute-start.1 = (bf16[1024,1152]{1,0:T(8,128)(2,1)S(1)}, bf16[1024,1152]{1,0:T(8,128)(2,1)S(1)}, u32[]{:S(2)}, u32[]{:S(2)}) collective-permute-start(bf16[1024,1152]{1,0:T(8,128)(2,1)S(1)} %convolution_convert_fusion), channel_id=1, source_target_pairs={{1,0},{2,1},{3,2},{4,3},{5,4},{6,5},{7,6},{8,7},{9,8},{10,9},{11,1... | collective-permute-start | bytes 7077896 | tf_op jit(solution)/shard_map/ppermute | solution.py:12
  53.5 21.9 %copy-start = (bf16[1024,1152]{1,0:T(8,128)(2,1)S(1)}, bf16[1024,1152]{1,0:T(8,128)(2,1)}, u32[]{:S(2)}) copy-start(bf16[1024,1152]{1,0:T(8,128)(2,1)} %param.5) | copy-start | bytes 7077892
where the time goes:
time: 81.7 us; the launch traced here: 81.5 us
  waiting for transfers between devices  42.1 us (52%)
  matrix products  26.3 us (32%)
  other arithmetic  10.7 us (13%)
  between operations  2.01 us (2%)
    ppermute x2, waiting for transfers between devices, passed_along(): return lax.ppermute(block, axis, route)  42.1 us
    dot_general x2, matrix products, tile_penalty_parts(): jnp.einsum('id,jd->ij', preceding_device, following_device, preferred_ele...  12.5 us
    dot_general x2, matrix products, shards(): jnp.einsum('ij,id->jd', derivative_multiplier, picture_summed_share, pref...  7.04 us
    convert_element_type x2, other arithmetic, unit_backward(): return ((grad - unit * along) / size).astype(jnp.bfloat16)  4.75 us
    dot_general x1, matrix products, shards(): jnp.dot(derivative_multiplier, counterpart_slice, preferred_element_type=...  3.8 us
    dot_general x1, matrix products, shards(): jnp.dot(derivative_multiplier, caption_summed_share, preferred_element_ty...  2.97 us
    reduce_sum x2, other arithmetic, normalize(): size = jnp.sqrt(jnp.sum(wide * wide, axis=-1, keepdims=True) + 1e-06)  2.87 us
    convert_element_type x1, other arithmetic, shards(): caption_summed_share = text_unit.astype(jnp.bfloat16)  2.42 us
  transfers between devices with their start and end apart: 2, of which 2 were waited for; matrix products, arithmetic and copies ran while one was open for 22% of the time, Pallas kernels for 0%

commit v1 on v0

v1 whole, which is shorter than its diff:
```python
import functools
import math

import jax
import jax.numpy as jnp
from jax import lax
from jax.experimental import pallas as pl
from jax.experimental.pallas import tpu as pltpu
from jax.sharding import PartitionSpec as P

ROUNDS = 2
EPS = 1e-06
LOG2E = 1.0 / math.log(2.0)
LN2 = math.log(2.0)
TILE = 256
MESH = pl.DeviceIdType.MESH
F32 = jnp.float32
BF16 = jnp.bfloat16


def dot_nt(a, b):
    return lax.dot_general(a, b, (((1,), (1,)), ((), ())), preferred_element_type=F32)


def dot_nn(a, b):
    return lax.dot_general(a, b, (((1,), (0,)), ((), ())), preferred_element_type=F32)


def softplus_and_coeff(exponent, scale):
    e = jnp.exp2(exponent)
    one = 1.0 + e
    small = e * (1.0 - e * (0.5 - e * (1.0 / 3.0)))
    loss = jnp.where(e < 0.002, small, jnp.log(one))
    coeff = (e / one) * scale
    return loss, coeff


def lane_groups(x):
    total = x[:, :128]
    for k in range(1, x.shape[1] // 128):
        total = total + x[:, k * 128 : (k + 1) * 128]
    return total


def sublane_groups(x):
    return jnp.sum(x.reshape(x.shape[0] // 8, 8, x.shape[1]), axis=0)


def normalize_rows(raw, low, inv, rows):
    x = raw[rows, :].astype(F32)
    size = jnp.sqrt(jnp.sum(x * x, axis=-1, keepdims=True) + EPS)
    recip = 1.0 / size
    low[rows, :] = (x * recip).astype(BF16)
    inv[rows, :] = jnp.broadcast_to(recip, (recip.shape[0], 128))


def project(grad, raw, inv, rows):
    recip = inv[rows, :][:, :1]
    unit = raw[rows, :].astype(F32) * recip
    along = jnp.sum(unit * grad, axis=-1, keepdims=True)
    return ((grad - unit * along) * recip).astype(BF16)


def pair_kernel(
    img, txt, scale_ref, shift_ref,
    loss_o, ga_o, gb_o,
    ar, br, al, bl, ys, yf, ct, da, ainv, binv, la, lb, lcol,
    lsa, lsb, ssend, srecv, fsend, frecv,
):
    pairs = ar.shape[0]
    nt = pairs // TILE
    me = lax.axis_index("dp")
    n = lax.axis_size("dp")
    parity = lax.rem(me, 2)
    slow = lax.rem(me + n - 1 + 2 * parity, n)
    fast = me + 1 - 2 * parity

    barrier = pltpu.get_barrier_semaphore()
    for partner in (slow, fast):
        pl.semaphore_signal(barrier, inc=1, device_id=(partner,), device_id_type=MESH)

    def chunk(i):
        return pl.ds(i * TILE, TILE)

    def load(src, dst, sem, i):
        return pltpu.make_async_copy(src.at[chunk(i)], dst.at[chunk(i)], sem.at[i])

    def send_slow(i):
        return pltpu.make_async_remote_copy(
            al.at[chunk(i)], ys.at[chunk(i)], ssend.at[i], srecv.at[i], (slow,), MESH
        )

    def send_fast(i):
        return pltpu.make_async_remote_copy(
            bl.at[chunk(i)], yf.at[chunk(i)], fsend.at[i], frecv.at[i], (fast,), MESH
        )

    @pl.when(parity == 0)
    def _():
        for i in range(nt):
            load(img, ar, lsa, i).start()
        for i in range(nt):
            load(txt, br, lsb, i).start()

    @pl.when(parity == 1)
    def _():
        for i in range(nt):
            load(txt, ar, lsa, i).start()
        for i in range(nt):
            load(img, br, lsb, i).start()

    for i in range(nt):
        load(img, ar, lsa, i).wait()
        normalize_rows(ar, al, ainv, chunk(i))
    pl.semaphore_wait(barrier, 2)
    for i in range(nt):
        send_slow(i).start()
    for i in range(nt):
        load(img, br, lsb, i).wait()
        normalize_rows(br, bl, binv, chunk(i))
        send_fast(i).start()

    lcol[...] = jnp.zeros_like(lcol)
    scale = scale_ref[0]
    scale2 = scale * LOG2E
    shift2 = shift_ref[0] * LOG2E

    for i in range(nt):
        rows = chunk(i)
        exponent = dot_nt(al[rows, :], bl[...]) * scale2 + shift2
        r = lax.broadcasted_iota(jnp.int32, exponent.shape, 0) + i * TILE
        c = lax.broadcasted_iota(jnp.int32, exponent.shape, 1)
        match = r == c
        exponent = jnp.where(match, -exponent, exponent)
        loss, coeff = softplus_and_coeff(exponent, jnp.where(match, -scale, scale))
        la[rows, :] = lane_groups(loss)
        lcol[...] += sublane_groups(loss)
        low = coeff.astype(BF16)
        ct[:, rows] = low.T
        da[rows, :] = dot_nn(low, bl[...])

    for i in range(nt):
        send_fast(i).wait_recv()

    for j in range(nt):
        rows = chunk(j)
        exponent = dot_nt(bl[rows, :], yf[...]) * scale2 + shift2
        loss, coeff = softplus_and_coeff(exponent, scale)
        lb[rows, :] = lane_groups(loss)
        grad = dot_nn(ct[rows, :], al[...]) + dot_nn(coeff.astype(BF16), yf[...])
        gb_o[rows, :] = project(grad, br, binv, rows)

    for c in range(nt):
        send_slow(c).wait_recv()

        block = ys[chunk(c), :]
        for i in range(nt):
            rows = chunk(i)
            exponent = dot_nt(al[rows, :], block) * scale2 + shift2
            loss, coeff = softplus_and_coeff(exponent, scale)
            la[rows, :] += lane_groups(loss)
            grad = da[rows, :] + dot_nn(coeff.astype(BF16), block)
            if c < nt - 1:
                da[rows, :] = grad
            else:
                ga_o[rows, :] = project(grad, ar, ainv, rows)

    mean = 1.0 / (ROUNDS * pairs)

    @pl.when(parity == 0)
    def _():
        for k in range(pairs // 128):
            block = la[k * 128 : (k + 1) * 128, :].T
            loss_o[k : k + 1, :] = jnp.sum(block, axis=0, keepdims=True) * mean

    @pl.when(parity == 1)
    def _():
        for k in range(pairs // 128):
            block = lb[k * 128 : (k + 1) * 128, :].T
            own = jnp.sum(lcol[:, k * 128 : (k + 1) * 128], axis=0, keepdims=True)
            loss_o[k : k + 1, :] = (jnp.sum(block, axis=0, keepdims=True) + own) * mean

    for i in range(nt):
        send_fast(i).wait_send()
    for i in range(nt):
        send_slow(i).wait_send()


def place_kernel(loss, ga, gb, loss_o, gimg_o, gtxt_o, sems):
    parity = lax.rem(lax.axis_index("dp"), 2)

    @pl.when(parity == 0)
    def _():
        pltpu.make_async_copy(ga, gimg_o, sems.at[0]).start()
        pltpu.make_async_copy(gb, gtxt_o, sems.at[1]).start()

    @pl.when(parity == 1)
    def _():
        pltpu.make_async_copy(gb, gimg_o, sems.at[0]).start()
        pltpu.make_async_copy(ga, gtxt_o, sems.at[1]).start()

    last = pltpu.make_async_copy(loss, loss_o, sems.at[2])
    last.start()
    pltpu.make_async_copy(ga, gimg_o, sems.at[0]).wait()
    pltpu.make_async_copy(gb, gtxt_o, sems.at[1]).wait()
    last.wait()


def shards(img, txt, scale, shift):
    pairs, width = img.shape
    nt = pairs // TILE
    hbm_spec = pl.BlockSpec(memory_space=pltpu.HBM)
    smem_spec = pl.BlockSpec(memory_space=pltpu.SMEM)
    vmem_spec = pl.BlockSpec(memory_space=pltpu.VMEM)
    block = pltpu.VMEM((pairs, width), BF16)
    loss, ga, gb = pl.pallas_call(
        pair_kernel,
        out_shape=(
            pltpu.VMEM((pairs // 128, 128), F32),
            pltpu.VMEM((pairs, width), BF16),
            pltpu.VMEM((pairs, width), BF16),
        ),
        in_specs=[hbm_spec, hbm_spec, smem_spec, smem_spec],
        out_specs=(vmem_spec, vmem_spec, vmem_spec),
        scratch_shapes=[
            block, block, block, block, block, block,
            pltpu.VMEM((pairs, pairs), BF16),
            pltpu.VMEM((pairs, width), F32),
            pltpu.VMEM((pairs, 128), F32),
            pltpu.VMEM((pairs, 128), F32),
            pltpu.VMEM((pairs, 128), F32),
            pltpu.VMEM((pairs, 128), F32),
            pltpu.VMEM((8, pairs), F32),
        ]
        + [pltpu.SemaphoreType.DMA((nt,))] * 6,
        compiler_params=pltpu.CompilerParams(
            collective_id=0, has_side_effects=True, vmem_limit_bytes=44 * 2**20
        ),
        name="pair_tiles",
    )(
        pltpu.with_memory_space_constraint(img, pltpu.HBM),
        pltpu.with_memory_space_constraint(txt, pltpu.HBM),
        scale,
        shift,
    )
    loss, gimg, gtxt = pl.pallas_call(
        place_kernel,
        out_shape=(
            jax.ShapeDtypeStruct(loss.shape, F32),
            jax.ShapeDtypeStruct(img.shape, BF16),
            jax.ShapeDtypeStruct(txt.shape, BF16),
        ),
        in_specs=[vmem_spec] * 3,
        out_specs=(hbm_spec, hbm_spec, hbm_spec),
        scratch_shapes=[pltpu.SemaphoreType.DMA((3,))],
        compiler_params=pltpu.CompilerParams(vmem_limit_bytes=2**20),
        name="place_outputs",
    )(*(pltpu.with_memory_space_constraint(x, pltpu.VMEM) for x in (loss, ga, gb)))
    return loss.reshape(pairs), gimg, gtxt


def solution(mesh):
    in_specs = (P("dp", None), P("dp", None), P(), P())
    out_specs = (P("dp"), P("dp", None), P("dp", None))
    return jax.shard_map(shards, mesh=mesh, in_specs=in_specs, out_specs=out_specs, check_vma=False)
```

time: 81.7 us -> 45.6 us (0.56)
  Pallas kernels: 0 us -> 43.4 us
  waiting for transfers between devices: 42.1 us -> 0 us
  matrix products: 26.3 us -> 0 us
  other arithmetic: 10.7 us -> 0 us
    pallas_call x0 -> x2, Pallas kernels: none -> 43.4 us  [the longest x1 41.2 us: shards(): pl.pallas_call(pair_kernel, out_shape=(pltpu.VMEM((pairs // 128, 128), F3...]
    ppermute x2 -> x0, waiting for transfers between devices: 42.1 us -> none  [passed_along(): return lax.ppermute(block, axis, route)]
    dot_general x6 -> x0, matrix products: 26.3 us -> none  [the longest x2 12.5 us: tile_penalty_parts(): jnp.einsum('id,jd->ij', preceding_device, following_device, preferred_ele...]
    convert_element_type x3 -> x0, other arithmetic: 7.17 us -> none  [the longest x2 4.75 us: unit_backward(): return ((grad - unit * along) / size).astype(jnp.bfloat16)]
    reduce_sum x2 -> x0, other arithmetic: 2.87 us -> none  [normalize(): size = jnp.sqrt(jnp.sum(wide * wide, axis=-1, keepdims=True) + 1e-06)]
  transfers between devices with their start and end apart: 2 -> 0, of which waited for: 2 -> 0; matrix products, arithmetic and copies ran while one was open for 22% -> 0% of each run, Pallas kernels for 0% -> 0%
where the time goes in v1:
time: 45.6 us; the launch traced here: 45.5 us
  Pallas kernels  43.4 us (95%)
  between operations  2.09 us (5%)
    pallas_call x1, Pallas kernels, shards(): pl.pallas_call(pair_kernel, out_shape=(pltpu.VMEM((pairs // 128, 128), F3...  41.2 us
    pallas_call x1, Pallas kernels, shards(): pl.pallas_call(place_kernel, out_shape=(jax.ShapeDtypeStruct(loss.shape,...  2.22 us

profile of v1, /device:TPU:0, one launch (start us, length us, event | category | flops | bytes accessed | tf_op | source)
XLA Modules:
  0.0 45.5 jit_solution(9492865078361473505)
XLA Ops:
  1.9 41.2 %pair_tiles.1 = (f32[8,128]{1,0:T(8,128)S(1)}, bf16[1024,1152]{1,0:T(8,128)(2,1)S(1)}, bf16[1024,1152]{1,0:T(8,128)(2,1)S(1)}) custom-call(bf16[1024,1152]{1,0:T(8,128)(2,1)} %img.1, bf16[1024,1152]{1,0:T(8,128)(2,1)} %txt.1, f32[1]{0:T(128)S(6)} %copy.7.scale_ref, f32[1]{0:T(128)S(6)} %copy.8.shift_ref), custom_call_target="tpu_custom_call" | custom-call | tf_op jit(solution)/shard_map/pair_tiles/pallas_call | solution.py:216
  43.1 2.2 %place_outputs.1 = (f32[8,128]{1,0:T(8,128)}, bf16[1024,1152]{1,0:T(8,128)(2,1)}, bf16[1024,1152]{1,0:T(8,128)(2,1)}) custom-call(f32[8,128]{1,0:T(8,128)S(1)} %get-tuple-element.9.loss, bf16[1024,1152]{1,0:T(8,128)(2,1)S(1)} %get-tuple-element.10.ga, bf16[1024,1152]{1,0:T(8,128)(2,1)S(1)} %get-tuple-element.11.gb), custom_call_target="tpu_custom_call" | custom-call | tf_op jit(solution)/shard_map/place_outputs/pallas_call | solution.py:246

commit v2 on v1

v2 whole, which is shorter than its diff:
```python
import functools
import math

import jax
import jax.numpy as jnp
from jax import lax
from jax.experimental import pallas as pl
from jax.experimental.pallas import tpu as pltpu
from jax.sharding import PartitionSpec as P

ROUNDS = 2
EPS = 1e-06
LOG2E = 1.0 / math.log(2.0)
LN2 = math.log(2.0)
TILE = 256
SLOW_CHUNKS = ((0, 768), (768, 256))
LATE_EVERY = 64
LATE_TILE = 1
MESH = pl.DeviceIdType.MESH
F32 = jnp.float32
BF16 = jnp.bfloat16


def dot_nt(a, b):
    return lax.dot_general(a, b, (((1,), (1,)), ((), ())), preferred_element_type=F32)


def dot_nn(a, b):
    return lax.dot_general(a, b, (((1,), (0,)), ((), ())), preferred_element_type=F32)


def softplus_and_coeff(exponent, scale):
    e = jnp.exp2(exponent)
    one = 1.0 + e
    small = e * (1.0 - e * (0.5 - e * (1.0 / 3.0)))
    loss = jnp.where(e < 0.002, small, jnp.log(one))
    coeff = (e / one) * scale
    return loss, coeff


def lane_groups(x):
    total = x[:, :128]
    for k in range(1, x.shape[1] // 128):
        total = total + x[:, k * 128 : (k + 1) * 128]
    return total


def sublane_groups(x):
    return jnp.sum(x.reshape(x.shape[0] // 8, 8, x.shape[1]), axis=0)


def inverse_size(x):
    return 1.0 / jnp.sqrt(jnp.sum(x * x, axis=-1, keepdims=True) + EPS)


def row_of(partial, k):
    return jnp.sum(partial[k * 128 : (k + 1) * 128, :].T, axis=0, keepdims=True)


def normalize_rows(raw, low, rows, inv=None):
    x = raw[rows, :].astype(F32)
    recip = inverse_size(x)
    low[rows, :] = (x * recip).astype(BF16)
    if inv is not None:
        inv[rows, :] = jnp.broadcast_to(recip, (recip.shape[0], 128))


def project(grad, raw, inv, rows):
    recip = inv[rows, :][:, :1]
    unit = raw[rows, :].astype(F32) * recip
    along = jnp.sum(unit * grad, axis=-1, keepdims=True)
    return ((grad - unit * along) * recip).astype(BF16)


def pair_kernel(
    img, txt, scale_ref, shift_ref,
    odd_loss, gb_o, la, da, ar, al, ainv, last_low,
    br, bl, yr, ys, yf, ct, binv, lb, lcol,
    lsa, lsb, ssend, srecv, fsend, frecv,
):
    pairs = ar.shape[0]
    nt = pairs // TILE
    me = lax.axis_index("dp")
    n = lax.axis_size("dp")
    parity = lax.rem(me, 2)
    slow = lax.rem(me + n - 1 + 2 * parity, n)
    fast = me + 1 - 2 * parity

    barrier = pltpu.get_barrier_semaphore()
    for partner in (slow, fast):
        pl.semaphore_signal(barrier, inc=1, device_id=(partner,), device_id_type=MESH)

    def chunk(i):
        return pl.ds(i * TILE, TILE)

    def load(src, dst, sem, i):
        return pltpu.make_async_copy(src.at[chunk(i)], dst.at[chunk(i)], sem.at[i])

    def send_slow(i, src=img):
        return pltpu.make_async_remote_copy(
            src.at[pl.ds(*SLOW_CHUNKS[i])], yr.at[pl.ds(*SLOW_CHUNKS[i])], ssend.at[i], srecv.at[i], (slow,), MESH
        )

    def start_slow():
        @pl.when(parity == 0)
        def _():
            for i in range(len(SLOW_CHUNKS)):
                send_slow(i, img).start()

        @pl.when(parity == 1)
        def _():
            for i in range(len(SLOW_CHUNKS)):
                send_slow(i, txt).start()

    def send_fast(i):
        return pltpu.make_async_remote_copy(
            bl.at[chunk(i)], yf.at[chunk(i)], fsend.at[i], frecv.at[i], (fast,), MESH
        )

    @pl.when(parity == 0)
    def _():
        for i in range(nt):
            load(img, ar, lsa, i).start()
        for i in range(nt):
            load(txt, br, lsb, i).start()

    @pl.when(parity == 1)
    def _():
        for i in range(nt):
            load(txt, ar, lsa, i).start()
        for i in range(nt):
            load(img, br, lsb, i).start()

    late = lax.rem(me, LATE_EVERY) == 0

    @pl.when(jnp.logical_not(late))
    def _():
        pl.semaphore_wait(barrier, 2)
        start_slow()

    for i in range(nt):
        load(img, br, lsb, i).wait()
        normalize_rows(br, bl, chunk(i), binv)

    @pl.when(jnp.logical_not(late))
    def _():
        for i in range(nt):
            send_fast(i).start()

    for i in range(nt):
        load(img, ar, lsa, i).wait()
        normalize_rows(ar, al, chunk(i), ainv)

    lcol[...] = jnp.zeros_like(lcol)
    scale = scale_ref[0]
    scale2 = scale * LOG2E
    shift2 = shift_ref[0] * LOG2E

    for i in range(nt):
        rows = chunk(i)
        exponent = dot_nt(al[rows, :], bl[...]) * scale2 + shift2
        r = lax.broadcasted_iota(jnp.int32, exponent.shape, 0) + i * TILE
        c = lax.broadcasted_iota(jnp.int32, exponent.shape, 1)
        match = r == c
        exponent = jnp.where(match, -exponent, exponent)
        loss, coeff = softplus_and_coeff(exponent, jnp.where(match, -scale, scale))
        la[rows, :] = lane_groups(loss)
        lcol[...] += sublane_groups(loss)
        low = coeff.astype(BF16)
        ct[:, rows] = low.T
        da[rows, :] = dot_nn(low, bl[...])
        if i == LATE_TILE:

            @pl.when(late)
            def _():
                pl.semaphore_wait(barrier, 2)
                start_slow()
                for k in range(nt):
                    send_fast(k).start()


    for i in range(nt):
        send_fast(i).wait_recv()

    for j in range(nt):
        rows = chunk(j)
        exponent = dot_nt(bl[rows, :], yf[...]) * scale2 + shift2
        loss, coeff = softplus_and_coeff(exponent, scale)
        lb[rows, :] = lane_groups(loss)
        grad = dot_nn(ct[rows, :], al[...]) + dot_nn(coeff.astype(BF16), yf[...])
        gb_o[rows, :] = project(grad, br, binv, rows)

    mean = 1.0 / (ROUNDS * pairs)
    for k in range(pairs // 128):
        own = jnp.sum(lcol[:, k * 128 : (k + 1) * 128], axis=0, keepdims=True)
        odd_loss[k : k + 1, :] = (row_of(lb, k) + own) * mean

    for c, (first, count) in enumerate(SLOW_CHUNKS[:-1]):
        send_slow(c).wait_recv()
        part = pl.ds(first, count)
        normalize_rows(yr, ys, part)
        block = ys[part, :]
        for i in range(nt):
            rows = chunk(i)
            exponent = dot_nt(al[rows, :], block) * scale2 + shift2
            loss, coeff = softplus_and_coeff(exponent, scale)
            la[rows, :] += lane_groups(loss)
            da[rows, :] += dot_nn(coeff.astype(BF16), block)

    send_slow(len(SLOW_CHUNKS) - 1).wait_recv()
    last_rows = yr[pl.ds(*SLOW_CHUNKS[-1]), :].astype(F32)
    last_low[...] = (last_rows * inverse_size(last_rows)).astype(BF16)

    for i in range(nt):
        send_fast(i).wait_send()
    for i in range(len(SLOW_CHUNKS)):
        send_slow(i).wait_send()


def last_kernel(
    scale_ref, shift_ref, odd_loss, gb, la, da, ar, al, ainv, last_low,
    loss_o, gimg_o, gtxt_o,
    ga, rows_loss, sems,
):
    parity = lax.rem(lax.axis_index("dp"), 2)
    pairs = ga.shape[0]
    nt = pairs // TILE

    def place(src, dst, which, k):
        rows = pl.ds(k * TILE, TILE)
        return pltpu.make_async_copy(src.at[rows], dst.at[rows], sems.at[which, k])

    @pl.when(parity == 0)
    def _():
        for k in range(nt):
            place(gb, gtxt_o, 1, k).start()

    @pl.when(parity == 1)
    def _():
        for k in range(nt):
            place(gb, gimg_o, 1, k).start()

    scale = scale_ref[0]
    scale2 = scale * LOG2E
    shift2 = shift_ref[0] * LOG2E
    block = last_low[...]
    mean = 1.0 / (ROUNDS * pairs)
    lows = []
    for i in range(nt):
        rows = pl.ds(i * TILE, TILE)
        exponent = dot_nt(al[rows, :], block) * scale2 + shift2
        loss, coeff = softplus_and_coeff(exponent, scale)
        lows.append(coeff.astype(BF16))
        total = la[rows, :] + lane_groups(loss)
        for h in range(TILE // 128):
            k = i * (TILE // 128) + h
            even = row_of(total, h) * mean
            rows_loss[k : k + 1, :] = jnp.where(parity == 0, even, odd_loss[k : k + 1, :])
    loss_copy = pltpu.make_async_copy(rows_loss, loss_o, sems.at[2, 0])
    loss_copy.start()

    def start_place(k):
        @pl.when(parity == 0)
        def _():
            place(ga, gimg_o, 0, k).start()

        @pl.when(parity == 1)
        def _():
            place(ga, gtxt_o, 0, k).start()

    for i in range(nt):
        rows = pl.ds(i * TILE, TILE)
        grad = da[rows, :] + dot_nn(lows[i], block)
        ga[rows, :] = project(grad, ar, ainv, rows)
        start_place(i)

    for k in range(nt):
        place(ga, gimg_o, 0, k).wait()
        place(gb, gtxt_o, 1, k).wait()
    loss_copy.wait()


def shards(img, txt, scale, shift):
    pairs, width = img.shape
    nt = pairs // TILE
    hbm_spec = pl.BlockSpec(memory_space=pltpu.HBM)
    smem_spec = pl.BlockSpec(memory_space=pltpu.SMEM)
    vmem_spec = pl.BlockSpec(memory_space=pltpu.VMEM)
    block = pltpu.VMEM((pairs, width), BF16)
    partial = pltpu.VMEM((pairs, 128), F32)
    held = pl.pallas_call(
        pair_kernel,
        out_shape=(
            pltpu.VMEM((pairs // 128, 128), F32),
            block,
            partial,
            pltpu.VMEM((pairs, width), F32),
            block,
            block,
            partial,
            pltpu.VMEM((SLOW_CHUNKS[-1][1], width), BF16),
        ),
        in_specs=[hbm_spec, hbm_spec, smem_spec, smem_spec],
        out_specs=(vmem_spec,) * 8,
        scratch_shapes=[
            block, block, block, block, block,
            pltpu.VMEM((pairs, pairs), BF16),
            partial,
            partial,
            pltpu.VMEM((8, pairs), F32),
        ]
        + [pltpu.SemaphoreType.DMA((nt,))] * 2
        + [pltpu.SemaphoreType.DMA((len(SLOW_CHUNKS),))] * 2
        + [pltpu.SemaphoreType.DMA((nt,))] * 2,
        compiler_params=pltpu.CompilerParams(
            collective_id=0, has_side_effects=True, vmem_limit_bytes=32 * 2**20
        ),
        name="pair_tiles",
    )(
        pltpu.with_memory_space_constraint(img, pltpu.HBM),
        pltpu.with_memory_space_constraint(txt, pltpu.HBM),
        scale,
        shift,
    )
    loss, gimg, gtxt = pl.pallas_call(
        last_kernel,
        out_shape=(
            jax.ShapeDtypeStruct((pairs // 128, 128), F32),
            jax.ShapeDtypeStruct(img.shape, BF16),
            jax.ShapeDtypeStruct(txt.shape, BF16),
        ),
        in_specs=[smem_spec, smem_spec] + [vmem_spec] * 8,
        out_specs=(hbm_spec, hbm_spec, hbm_spec),
        scratch_shapes=[
            block,
            pltpu.VMEM((pairs // 128, 128), F32),
            pltpu.SemaphoreType.DMA((3, nt)),
        ],
        compiler_params=pltpu.CompilerParams(vmem_limit_bytes=16 * 2**20),
        name="last_tiles",
    )(scale, shift, *(pltpu.with_memory_space_constraint(x, pltpu.VMEM) for x in held))
    return loss.reshape(pairs), gimg, gtxt


def solution(mesh):
    in_specs = (P("dp", None), P("dp", None), P(), P())
    out_specs = (P("dp"), P("dp", None), P("dp", None))
    return jax.shard_map(shards, mesh=mesh, in_specs=in_specs, out_specs=out_specs, check_vma=False)
```

time: 45.6 us -> 42.4 us (0.930)
  Pallas kernels: 43.4 us -> 40.2 us
    pallas_call x1, Pallas kernels: 41.2 us -> 36.2 us  [shards(): pl.pallas_call(pair_kernel, out_shape=(pltpu.VMEM((pairs // 128, 128), F3...]
    pallas_call x1, Pallas kernels: 2.22 us -> 4 us  [shards(): pl.pallas_call(last_kernel, out_shape=(jax.ShapeDtypeStruct((pairs // 128...]
where the time goes in v2:
time: 42.4 us; the launch traced here: 42.3 us
  Pallas kernels  40.2 us (95%)
  between operations  2.11 us (5%)
    pallas_call x1, Pallas kernels, shards(): pl.pallas_call(pair_kernel, out_shape=(pltpu.VMEM((pairs // 128, 128), F3...  36.2 us
    pallas_call x1, Pallas kernels, shards(): pl.pallas_call(last_kernel, out_shape=(jax.ShapeDtypeStruct((pairs // 128...  4 us

profile of v2, /device:TPU:0, one launch (start us, length us, event | category | flops | bytes accessed | tf_op | source)
XLA Modules:
  0.0 42.3 jit_solution(4372607746940150492)
XLA Ops:
  1.9 36.2 %pair_tiles.1 = (f32[8,128]{1,0:T(8,128)S(1)}, bf16[1024,1152]{1,0:T(8,128)(2,1)S(1)}, f32[1024,128]{1,0:T(8,128)S(1)}, f32[1024,1152]{1,0:T(8,128)S(1)}, bf16[1...) custom-call(bf16[1024,1152]{1,0:T(8,128)(2,1)} %img.1, ...), custom_call_target="tpu_custom_call" | custom-call | tf_op jit(solution)/shard_map/pair_tiles/pallas_call | solution.py:291
  38.1 4.0 %last_tiles.1 = (f32[8,128]{1,0:T(8,128)}, bf16[1024,1152]{1,0:T(8,128)(2,1)}, bf16[1024,1152]{1,0:T(8,128)(2,1)}) custom-call(f32[1]{0:T(128)S(6)} %copy.7.scale_ref, f32[1]{0:T(128)S(6)} %copy.8.shift_ref, f32[8,128]{1,0:T(8,128)S(1)} %get-tuple-element.14.odd_loss, bf16[1024,1152]{1,0:T(8,128)(2,1)S(1)} %get-tuple-element.15.gb, ...), custom_call_target="tpu_custom_call" | custom-call | tf_op jit(solution)/shard_map/last_tiles/pallas_call | solution.py:325

commit v3 on v2

--- a/solution.py
+++ b/solution.py
@@ -13,7 +13,7 @@
 LOG2E = 1.0 / math.log(2.0)
 LN2 = math.log(2.0)
 TILE = 256
-SLOW_CHUNKS = ((0, 768), (768, 256))
+SLOW_CHUNKS = ((0, 640), (640, 256), (896, 128))
 LATE_EVERY = 64
 LATE_TILE = 1
 MESH = pl.DeviceIdType.MESH

time: 42.4 us -> 42.1 us (level)
  no operation moved by 1% of the time
where the time goes in v3:
time: 42.1 us; the launch traced here: 42 us
  Pallas kernels  39.9 us (95%)
  between operations  2.11 us (5%)
    pallas_call x1, Pallas kernels, shards(): pl.pallas_call(pair_kernel, out_shape=(pltpu.VMEM((pairs // 128, 128), F3...  36.3 us
    pallas_call x1, Pallas kernels, shards(): pl.pallas_call(last_kernel, out_shape=(jax.ShapeDtypeStruct((pairs // 128...  3.6 us

profile of v3, /device:TPU:0, one launch (start us, length us, event | category | flops | bytes accessed | tf_op | source)
XLA Modules:
  0.0 42.0 jit_solution(14279110588546664463)
XLA Ops:
  1.9 36.3 %pair_tiles.1 = (f32[8,128]{1,0:T(8,128)S(1)}, bf16[1024,1152]{1,0:T(8,128)(2,1)S(1)}, f32[1024,128]{1,0:T(8,128)S(1)}, f32[1024,1152]{1,0:T(8,128)S(1)}, bf16[1...) custom-call(bf16[1024,1152]{1,0:T(8,128)(2,1)} %img.1, ...), custom_call_target="tpu_custom_call" | custom-call | tf_op jit(solution)/shard_map/pair_tiles/pallas_call | solution.py:291
  38.2 3.6 %last_tiles.1 = (f32[8,128]{1,0:T(8,128)}, bf16[1024,1152]{1,0:T(8,128)(2,1)}, bf16[1024,1152]{1,0:T(8,128)(2,1)}) custom-call(f32[1]{0:T(128)S(6)} %copy.7.scale_ref, f32[1]{0:T(128)S(6)} %copy.8.shift_ref, f32[8,128]{1,0:T(8,128)S(1)} %get-tuple-element.14.odd_loss, bf16[1024,1152]{1,0:T(8,128)(2,1)S(1)} %get-tuple-element.15.gb, ...), custom_call_target="tpu_custom_call" | custom-call | tf_op jit(solution)/shard_map/last_tiles/pallas_call | solution.py:325
